TPU v7x, 512 devices: a whole 4x4x16 slice. The times are simulated.
512 devices in a mesh: ctx: 64 (over y, z_lo, core), head: 8 (over x, z_hi).
Axes of the slice: x: 4, y: 4, z: 16 (z_hi: 2, z_lo: 8; z = z_hi * 8 + z_lo), core: 2. Of those that a mesh axis runs over, the one named last changes fastest.
Arguments:
- q_first: bfloat16 [1024, 1024], P('ctx', 'head'), may hold values from -8 to 8
- q_second: bfloat16 [1024, 1024], P('ctx', 'head'), may hold values from -8 to 8
- grad_out: bfloat16 [1024, 2048], P('ctx', 'head'), may hold values from -6 to 6
- k_first: bfloat16 [65536, 1024], P('ctx', 'head'), may hold values from -4.5 to 4.5
- k_second: bfloat16 [65536, 1024], P('ctx', 'head'), may hold values from -4.5 to 4.5
- values: bfloat16 [65536, 2048], P('ctx', 'head'), may hold values from -6 to 6
- w_query: bfloat16 [4096, 2048], P(None, 'head'), may hold values from -0.09375 to 0.09375
- block_offsets: int32 [64], replicated, may hold values from 0 to 4095, as said below
- lambda_full: float32 [1], replicated, may hold values from 0.2 to 0.8
Outputs:
- grad_q_first: bfloat16 [1024, 1024], P('ctx', 'head')
- grad_q_second: bfloat16 [1024, 1024], P('ctx', 'head')
- grad_k_first: bfloat16 [65536, 1024], P('ctx', 'head')
- grad_k_second: bfloat16 [65536, 1024], P('ctx', 'head')
- grad_values: bfloat16 [65536, 2048], P('ctx', 'head')
- grad_slab_input: bfloat16 [1024, 4096], P('ctx', 'head')
Inputs may be any that keep to these rules, and one draw needn't show every extreme that they name: block_offsets[b] lies in [b * 64, (b + 1) * 64); the first is 0 and the last is 4095.
All inputs are finite; a program needn't handle non-finite values.
Results may differ from a plain program's by a relative error of at most 0.015.
Values may be sent and summed in bfloat16 or wider, within the bound.
No kernel may reach another device: no remote copies, remote signals or barrier semaphores. Data moves between devices by JAX's collectives and lax.ppermute only.
A program may use at most 64 MiB of HBM per device.

v0:
```python
import jax
import jax.numpy as jnp
from jax import lax
from jax.sharding import PartitionSpec as P

NEG = -1e30


def combined_all(value, axis, join):
    pieces = jax.tree.map(lambda part: lax.all_gather(part, axis), value)
    head = jax.tree.map(lambda part: part[0], pieces)
    tail = jax.tree.map(lambda part: part[1:], pieces)
    subtotal, _ = lax.scan(lambda subtotal, section: (join(subtotal, section), None), head, tail)
    return subtotal


def scores(queries, keys, visible, scale):
    raw = jnp.einsum("qd,kd->qk", queries, keys, preferred_element_type=jnp.float32) * scale
    return jnp.where(visible, raw, NEG)


def fold_totals(first, second):
    result = []
    for base in (0, 3):
        top = jnp.maximum(first[base], second[base])
        left = jnp.exp(first[base] - top)
        right = jnp.exp(second[base] - top)
        result = result + [
            top,
            first[base + 1] * left + second[base + 1] * right,
            first[base + 2] * left + second[base + 2] * right,
        ]
    return tuple(result)


def body(
    q_first, q_second, grad_out, k_first, k_second, values, w_query, block_offsets, lambda_full
):
    rows_local = q_first.shape[0]
    keys_local = k_first.shape[0]
    head_dim = q_first.shape[1]
    scale = head_dim ** (-0.5)
    weight = lambda_full[0]
    every_first, every_second, every_grad = (
        lax.all_gather(q_first, "ctx", axis=0, tiled=True),
        lax.all_gather(q_second, "ctx", axis=0, tiled=True),
        lax.all_gather(grad_out, "ctx", axis=0, tiled=True),
    )
    total_rows = every_first.shape[0]
    block = 512
    count = total_rows // block
    key_pos = lax.axis_index("ctx") * keys_local + jnp.arange(keys_local, dtype=jnp.int32)
    query_pos = (
        block_offsets[:, None] * rows_local + jnp.arange(rows_local, dtype=jnp.int32)[None, :]
    ).reshape(total_rows)
    pieces = (
        every_first.reshape(count, block, head_dim),
        every_second.reshape(count, block, head_dim),
        every_grad.reshape(count, block, 2 * head_dim),
        query_pos.reshape(count, block),
    )

    def local_totals(piece):
        part_a, part_b, part_grad, positions = piece
        visible = key_pos[None, :] <= positions[:, None]
        product = jnp.einsum("qe,ke->qk", part_grad, values, preferred_element_type=jnp.float32)
        result = []
        for queries, keys in ((part_a, k_first), (part_b, k_second)):
            logits = scores(queries, keys, visible, scale)
            top = jnp.max(logits, axis=1)
            expo = jnp.where(visible, jnp.exp(logits - top[:, None]), 0.0)
            result = result + [top, jnp.sum(expo, axis=1), jnp.sum(expo * product, axis=1)]
        return tuple(result)

    partial_totals = tuple((item.reshape(total_rows) for item in lax.map(local_totals, pieces)))
    top_a, sum_a, mix_a, top_b, sum_b, mix_b = combined_all(partial_totals, "ctx", fold_totals)
    delta_a = mix_a / sum_a
    delta_b = mix_b / sum_b
    totals = tuple(
        (item.reshape(count, block) for item in (top_a, sum_a, delta_a, top_b, sum_b, delta_b))
    )

    def gradient_block(carry, piece):
        grad_ka, grad_kb, grad_val = carry
        (
            part_a,
            part_b,
            part_grad,
            positions,
            top_one,
            sum_one,
            shift_one,
            top_two,
            sum_two,
            shift_two,
        ) = piece
        visible = key_pos[None, :] <= positions[:, None]
        product = jnp.einsum("qe,ke->qk", part_grad, values, preferred_element_type=jnp.float32)
        prob_a = jnp.where(
            visible,
            jnp.exp(scores(part_a, k_first, visible, scale) - top_one[:, None]) / sum_one[:, None],
            0.0,
        )
        prob_b = jnp.where(
            visible,
            jnp.exp(scores(part_b, k_second, visible, scale) - top_two[:, None]) / sum_two[:, None],
            0.0,
        )
        mixed = (prob_a - weight * prob_b).astype(jnp.bfloat16)
        slope_a = (prob_a * (product - shift_one[:, None]) * scale).astype(jnp.bfloat16)
        slope_b = (-weight * prob_b * (product - shift_two[:, None]) * scale).astype(jnp.bfloat16)
        grad_val = grad_val + jnp.einsum(
            "qk,qe->ke", mixed, part_grad, preferred_element_type=jnp.float32
        )
        grad_ka = grad_ka + jnp.einsum(
            "qk,qd->kd", slope_a, part_a, preferred_element_type=jnp.float32
        )
        grad_kb = grad_kb + jnp.einsum(
            "qk,qd->kd", slope_b, part_b, preferred_element_type=jnp.float32
        )
        query_part = jnp.concatenate(
            [
                jnp.dot(slope_a, k_first, preferred_element_type=jnp.float32),
                jnp.dot(slope_b, k_second, preferred_element_type=jnp.float32),
            ],
            axis=1,
        )
        return ((grad_ka, grad_kb, grad_val), query_part)

    start = (
        jnp.zeros((keys_local, head_dim), jnp.float32),
        jnp.zeros((keys_local, head_dim), jnp.float32),
        jnp.zeros((keys_local, 2 * head_dim), jnp.float32),
    )
    (grad_ka, grad_kb, grad_val), query_terms = lax.scan(gradient_block, start, pieces + totals)
    query_terms = query_terms.reshape(total_rows, 2 * head_dim)
    own_terms = lax.psum_scatter(query_terms, "ctx", scatter_dimension=0, tiled=True)
    grad_query = own_terms.astype(jnp.bfloat16)
    slab_term = jnp.einsum("qe,de->qd", grad_query, w_query, preferred_element_type=jnp.float32)
    slab = lax.psum_scatter(slab_term.astype(jnp.bfloat16), "head", scatter_dimension=1, tiled=True)
    return (
        grad_query[:, :head_dim],
        grad_query[:, head_dim:],
        grad_ka.astype(jnp.bfloat16),
        grad_kb.astype(jnp.bfloat16),
        grad_val.astype(jnp.bfloat16),
        slab,
    )


def solution(mesh):
    in_specs = (
        P("ctx", "head"),
        P("ctx", "head"),
        P("ctx", "head"),
        P("ctx", "head"),
        P("ctx", "head"),
        P("ctx", "head"),
        P(None, "head"),
        P(),
        P(),
    )
    out_specs = (
        P("ctx", "head"),
        P("ctx", "head"),
        P("ctx", "head"),
        P("ctx", "head"),
        P("ctx", "head"),
        P("ctx", "head"),
    )
    return jax.shard_map(body, mesh=mesh, in_specs=in_specs, out_specs=out_specs, check_vma=False)
```

profile of v0, /device:TPU:24, one launch (start us, length us, event | category | flops | bytes accessed | tf_op | source)
XLA Modules:
  0.0 1770.3 jit_solution(14336723057849562854)
XLA Ops:
  8.4 120.3 %all_gather.27 = bf16[1024,128]{1,0:T(8,128)(2,1)} all-gather(bf16[16,128]{1,0:T(8,128)(2,1)} %param.15), channel_id=1, replica_groups=mesh['ctx'=64,'head'=8] {'ctx'}, dimensions={0}, use_global_device_ids=true | all-gather | bytes 266240 | tf_op jit(solution)/shard_map/all_gather | solution.py:45
  128.7 109.1 %all_gather.29 = bf16[1024,128]{1,0:T(8,128)(2,1)} all-gather(bf16[16,128]{1,0:T(8,128)(2,1)} %param.16), channel_id=1, replica_groups=mesh['ctx'=64,'head'=8] {'ctx'}, dimensions={0}, use_global_device_ids=true | all-gather | bytes 266240 | tf_op jit(solution)/shard_map/all_gather | solution.py:46
  237.8 111.6 %all_gather.28 = bf16[1024,256]{1,0:T(8,128)(2,1)} all-gather(bf16[16,256]{1,0:T(8,128)(2,1)} %param.17), channel_id=1, replica_groups=mesh['ctx'=64,'head'=8] {'ctx'}, dimensions={0}, use_global_device_ids=true | all-gather | bytes 532480 | tf_op jit(solution)/shard_map/all_gather | solution.py:47
  349.4 12.9 while.60
  352.8 2.8 multiply_reduce_fusion.3
  359.3 2.8 multiply_reduce_fusion.3
  362.4 112.5 %all-gather.4 = f32[64,1,1024]{2,1,0:T(1,128)S(1)} all-gather(f32[1,1,1024]{2,1,0:T(1,128)S(1)} %reshape.86), channel_id=1, replica_groups=mesh['ctx'=64,'head'=8] {'ctx'}, dimensions={0}, use_global_device_ids=true | all-gather | bytes 266240 | tf_op jit(solution)/shard_map/all_gather | solution.py:10
  474.9 114.6 %all-gather.3 = f32[64,1,1024]{2,1,0:T(1,128)S(1)} all-gather(f32[1,1,1024]{2,1,0:T(1,128)S(1)} %reshape.84), channel_id=1, replica_groups=mesh['ctx'=64,'head'=8] {'ctx'}, dimensions={0}, use_global_device_ids=true | all-gather | bytes 266240 | tf_op jit(solution)/shard_map/all_gather | solution.py:10
  589.5 113.7 %all-gather.2 = f32[64,1,1024]{2,1,0:T(1,128)S(1)} all-gather(f32[1,1,1024]{2,1,0:T(1,128)S(1)} %reshape.82), channel_id=1, replica_groups=mesh['ctx'=64,'head'=8] {'ctx'}, dimensions={0}, use_global_device_ids=true | all-gather | bytes 266240 | tf_op jit(solution)/shard_map/all_gather | solution.py:10
  703.9 114.6 %all-gather.1 = f32[64,1,1024]{2,1,0:T(1,128)S(1)} all-gather(f32[1,1,1024]{2,1,0:T(1,128)S(1)} %reshape.80), channel_id=1, replica_groups=mesh['ctx'=64,'head'=8] {'ctx'}, dimensions={0}, use_global_device_ids=true | all-gather | bytes 266240 | tf_op jit(solution)/shard_map/all_gather | solution.py:10
  819.3 113.7 %all-gather = f32[64,1,1024]{2,1,0:T(1,128)S(1)} all-gather(f32[1,1,1024]{2,1,0:T(1,128)S(1)} %reshape.78), channel_id=1, replica_groups=mesh['ctx'=64,'head'=8] {'ctx'}, dimensions={0}, use_global_device_ids=true | all-gather | bytes 266240 | tf_op jit(solution)/shard_map/all_gather | solution.py:10
  933.7 114.7 %all-gather.5 = f32[64,1,1024]{2,1,0:T(1,128)S(1)} all-gather(f32[1,1,1024]{2,1,0:T(1,128)S(1)} %reshape.88), channel_id=1, replica_groups=mesh['ctx'=64,'head'=8] {'ctx'}, dimensions={0}, use_global_device_ids=true | all-gather | bytes 266240 | tf_op jit(solution)/shard_map/all_gather | solution.py:10
  1054.3 107.6 %while.59 = (s32[]{:T(128)}, f32[1024]{0:T(1024)S(1)}, f32[1024]{0:T(1024)S(1)}, f32[1024]{0:T(1024)S(1)}, f32[1024]{0:T(1024)S(1)}, /*index=5*/f32[1024]{0:T(10...) while((s32[]{:T(128)}, f32[1024]{0:T(1024)S(1)}, ...), condition=%wide.region_9.10_spmd, body=%wide.region_8.9_spmd.sunk | while | flops 22530 | bytes 164001 | solution.py:13
  1162.0 33.0 %while.61 = (s32[]{:T(128)}, f32[1024,128]{1,0:T(8,128)}, f32[1024,128]{1,0:T(8,128)}, f32[1024,256]{1,0:T(8,128)}, f32[2,512,256]{2,1,0:T(8,128)}, /*index=5*/s...) while((s32[]{:T(128)}, f32[1024,128]{1,0:T(8,128)}, ...), condition=%wide.region_11.12_spmd.clone, body=%wide.region_10.11_spmd.clone.sunk | while | flops 1355940864 | bytes 29418768 | solution.py:135
  1165.5 3.3 convolution_add_fusion.8
  1171.2 2.2 convolution_add_fusion.6
  1174.8 2.2 convolution_add_fusion.7
  1181.6 3.6 convolution_add_fusion.8
  1185.2 1.9 multiply_convert_fusion.3
  1187.7 2.4 convolution_add_fusion.6
  1191.5 2.4 convolution_add_fusion.7
  1195.0 424.4 %reduce-scatter.3.cloned.1.call-done = f32[16,256]{1,0:T(8,128)} async-done(((f32[1024,256]{1,0:T(8,128)}), f32[16,256]{1,0:T(8,128)}) %reduce-scatter.3.cloned.1.call-update) | async-done | bytes 16400 | tf_op jit(solution)/shard_map/reduce_scatter | solution.py:137
  1625.1 2.1 convert_element_type.30
  1627.8 135.7 %reduce-scatter.5.cloned.1.call-done = bf16[16,512]{1,0:T(8,128)(2,1)} async-done(((bf16[16,4096]{1,0:T(8,128)(2,1)}), bf16[16,512]{1,0:T(8,128)(2,1)}) %reduce-scatter.5.cloned.1.call-update) | async-done | bytes 16400 | tf_op jit(solution)/shard_map/reduce_scatter | solution.py:140
  (747 shorter events, 140.0 us)
Async XLA Ops:
  7.2 1613.0 %copy-start = (bf16[4096,256]{1,0:T(8,128)(2,1)S(1)}, bf16[4096,256]{1,0:T(8,128)(2,1)}, u32[]{:S(2)}) copy-start(bf16[4096,256]{1,0:T(8,128)(2,1)} %param.21) | copy-start | bytes 6291460
  7.2 1612.3 %reduce-scatter.3.cloned.1.call-start = ((), (), s32[]{:S(2)}) async-start(), calls=%async_computation.2 | async-start | bytes 1064960 | tf_op jit(solution)/shard_map/reduce_scatter | solution.py:137
  474.8 574.4 %copy-start.2 = (f32[64,1,1024]{2,1,0:T(1,128)}, f32[64,1,1024]{2,1,0:T(1,128)S(1)}, u32[]{:S(2)}) copy-start(f32[64,1,1024]{2,1,0:T(1,128)S(1)} %all-gather.4) | copy-start | bytes 786436
  589.4 461.2 %copy-start.3 = (f32[64,1,1024]{2,1,0:T(1,128)}, f32[64,1,1024]{2,1,0:T(1,128)S(1)}, u32[]{:S(2)}) copy-start(f32[64,1,1024]{2,1,0:T(1,128)S(1)} %all-gather.3) | copy-start | bytes 786436
  1049.2 5.0 slice-start
  1049.9 4.2 copy-start.4
  1049.9 4.3 copy-start.5
  1049.9 112.1 %copy-start.1 = (bf16[1024,128]{1,0:T(8,128)(2,1)S(1)}, bf16[1024,128]{1,0:T(8,128)(2,1)}, u32[]{:S(2)}) copy-start(bf16[1024,128]{1,0:T(8,128)(2,1)} %get-tuple-element.1096) | copy-start | bytes 786436
  1051.4 2.8 slice-start.1
  1195.0 568.5 %reduce-scatter.5.cloned.1.call-start = ((), (), s32[]{:S(2)}) async-start(), calls=%async_computation.3 | async-start | bytes 147456 | tf_op jit(solution)/shard_map/reduce_scatter | solution.py:140
Sparse Core Ops, SparseCore 0:
  1195.1 424.3 reduce-scatter.2
  1625.1 138.3 reduce-scatter.4
where the time goes:
time: 1780 us; the launch traced here: 1770 us
  blocking collectives  1020 us (57%)
  waiting for transfers between devices  560 us (31%)
  local copies, waits for them, and re-layouts  112 us (6%)
  matrix products  44.2 us (2%)
    all_gather x6, blocking collectives, combined_all(): pieces = jax.tree.map(lambda part: lax.all_gather(part, axis), value)  684 us
    reduce_scatter x1, waiting for transfers between devices, body(): lax.psum_scatter(query_terms, 'ctx', scatter_dimension=0, tiled=True)  424 us
    reduce_scatter x1, waiting for transfers between devices, body(): lax.psum_scatter(slab_term.astype(jnp.bfloat16), 'head', scatter_dimensio...  136 us
    all_gather x1, blocking collectives, body(): lax.all_gather(q_first, 'ctx', axis=0, tiled=True)  120 us
    all_gather x1, blocking collectives, body(): lax.all_gather(grad_out, 'ctx', axis=0, tiled=True)  112 us
    all_gather x1, blocking collectives, body(): lax.all_gather(q_second, 'ctx', axis=0, tiled=True)  109 us
    dynamic_slice x315, local copies, waits for them, and re-layouts, combined_all(): lax.scan(lambda subtotal, section: (join(subtotal, section), None), head,...  100 us
  transfers between devices with their start and end apart: 2, of which 2 were waited for; matrix products, arithmetic and copies ran while one was open for 0% of the time, Pallas kernels for 0%

commit v1 on v0

v1 whole, which is shorter than its diff:
```python
import jax
import jax.numpy as jnp
from jax import lax
from jax.experimental import pallas as pl
from jax.experimental.pallas import tpu as pltpu
from jax.sharding import Mesh, PartitionSpec as P

NEG = -1e30
KEY_TILE = 256
ROW_TILE = 256
VMEM = pltpu.CompilerParams(
    dimension_semantics=("arbitrary",), vmem_limit_bytes=40 * 1024 * 1024
)

MAPS = (0, 4)


def outer(left, right):
    return lax.dot_general(
        left, right, (((1,), (1,)), ((), ())), preferred_element_type=jnp.float32
    )


def matmul(left, right):
    return jnp.dot(left, right, preferred_element_type=jnp.float32)


def matmul_first(left, right):
    return lax.dot_general(
        left, right, (((0,), (0,)), ((), ())), preferred_element_type=jnp.float32
    )


def tiles(total, size):
    size = min(size, total)
    return [(start, size) for start in range(0, total, size)]


def stats_kernel(base_ref, pos_ref, every_ref, k_one_ref, k_two_ref, val_ref, stats_ref):
    head_dim = k_one_ref.shape[1]
    scale = head_dim**-0.5
    tile = k_one_ref.shape[0]
    step = pl.program_id(0)

    @pl.when(step == 0)
    def _():
        row = lax.broadcasted_iota(jnp.int32, stats_ref.shape, 0)
        stats_ref[...] = jnp.where((row == 0) | (row == 4), NEG, 0.0)

    base = base_ref[0] + step * tile
    for start, width in tiles(every_ref.shape[0], ROW_TILE):
        span = slice(start, start + width)
        key_pos = base + lax.broadcasted_iota(jnp.int32, (tile, width), 0)
        visible = key_pos <= pos_ref[:, span]
        product = outer(val_ref[...], every_ref[span, 2 * head_dim :])
        for row, k_ref, offset in ((0, k_one_ref, 0), (4, k_two_ref, head_dim)):
            logits = outer(k_ref[...], every_ref[span, offset : offset + head_dim]) * scale
            logits = jnp.where(visible, logits, NEG)
            before = stats_ref[row : row + 1, span]
            top = jnp.maximum(before, jnp.max(logits, axis=0, keepdims=True))
            expo = jnp.exp(logits - top)
            kept = jnp.exp(before - top)
            stats_ref[row : row + 1, span] = top
            stats_ref[row + 1 : row + 2, span] = stats_ref[
                row + 1 : row + 2, span
            ] * kept + jnp.sum(expo, axis=0, keepdims=True)
            stats_ref[row + 2 : row + 3, span] = stats_ref[
                row + 2 : row + 3, span
            ] * kept + jnp.sum(expo * product, axis=0, keepdims=True)


def grad_kernel(
    base_ref,
    lam_ref,
    pos_ref,
    stats_ref,
    every_ref,
    k_one_ref,
    k_two_ref,
    val_ref,
    dk_one_ref,
    dk_two_ref,
    dval_ref,
    dq_ref,
    final_ref,
    acc_ref,
):
    head_dim = k_one_ref.shape[1]
    scale = head_dim**-0.5
    tile = k_one_ref.shape[0]
    step = pl.program_id(0)
    lam = lam_ref[0]

    @pl.when(step == 0)
    def _():
        for row in MAPS:
            top = jnp.max(stats_ref[:, row, :], axis=0, keepdims=True)
            total = jnp.zeros_like(top)
            mix = jnp.zeros_like(top)
            for part in range(stats_ref.shape[0]):
                kept = jnp.exp(stats_ref[part, row : row + 1, :] - top)
                total = total + kept * stats_ref[part, row + 1 : row + 2, :]
                mix = mix + kept * stats_ref[part, row + 2 : row + 3, :]
            final_ref[row : row + 1, :] = top + jnp.log(total)
            final_ref[row + 1 : row + 2, :] = mix / total
        acc_ref[...] = jnp.zeros_like(acc_ref)

    base = base_ref[0] + step * tile
    grad_one = jnp.zeros((tile, head_dim), jnp.float32)
    grad_two = jnp.zeros((tile, head_dim), jnp.float32)
    grad_val = jnp.zeros((tile, 2 * head_dim), jnp.float32)
    for start, width in tiles(every_ref.shape[0], ROW_TILE):
        span = slice(start, start + width)
        key_pos = base + lax.broadcasted_iota(jnp.int32, (tile, width), 0)
        visible = key_pos <= pos_ref[:, span]
        q_one = every_ref[span, :head_dim]
        q_two = every_ref[span, head_dim : 2 * head_dim]
        cotangent = every_ref[span, 2 * head_dim :]
        product = outer(val_ref[...], cotangent)
        logits_one = jnp.where(visible, outer(k_one_ref[...], q_one) * scale, NEG)
        logits_two = jnp.where(visible, outer(k_two_ref[...], q_two) * scale, NEG)
        prob_one = jnp.exp(logits_one - final_ref[0:1, span])
        prob_two = jnp.exp(logits_two - final_ref[4:5, span]) * lam
        mixed = (prob_one - prob_two).astype(jnp.bfloat16)
        slope_one = (prob_one * (product - final_ref[1:2, span]) * scale).astype(jnp.bfloat16)
        slope_two = (prob_two * (final_ref[5:6, span] - product) * scale).astype(jnp.bfloat16)
        grad_val = grad_val + matmul(mixed, cotangent)
        grad_one = grad_one + matmul(slope_one, q_one)
        grad_two = grad_two + matmul(slope_two, q_two)
        acc_ref[span, :head_dim] += matmul_first(slope_one, k_one_ref[...])
        acc_ref[span, head_dim:] += matmul_first(slope_two, k_two_ref[...])
    dk_one_ref[...] = grad_one.astype(jnp.bfloat16)
    dk_two_ref[...] = grad_two.astype(jnp.bfloat16)
    dval_ref[...] = grad_val.astype(jnp.bfloat16)

    @pl.when(step == pl.num_programs(0) - 1)
    def _():
        dq_ref[...] = acc_ref[...].astype(jnp.bfloat16)


def whole(shape):
    return pl.BlockSpec(shape, lambda step: (0,) * len(shape))


def keyed(width):
    return pl.BlockSpec((KEY_TILE, width), lambda step: (step, 0))


def local_stats(base, positions, every, k_first, k_second, values):
    rows, keys, head_dim = every.shape[0], k_first.shape[0], k_first.shape[1]
    smem = pl.BlockSpec(memory_space=pltpu.SMEM)
    return pl.pallas_call(
        stats_kernel,
        grid=(keys // KEY_TILE,),
        out_shape=jax.ShapeDtypeStruct((8, rows), jnp.float32),
        in_specs=[
            smem,
            whole((1, rows)),
            whole(every.shape),
            keyed(head_dim),
            keyed(head_dim),
            keyed(2 * head_dim),
        ],
        out_specs=whole((8, rows)),
        compiler_params=VMEM,
        cost_estimate=pl.CostEstimate(
            flops=8 * rows * keys * head_dim,
            bytes_accessed=2 * 4 * head_dim * (rows + keys),
            transcendentals=2 * rows * keys,
        ),
    )(base, positions, every, k_first, k_second, values)


def local_grads(base, lam, positions, stats, every, k_first, k_second, values):
    rows, keys, head_dim = every.shape[0], k_first.shape[0], k_first.shape[1]
    smem = pl.BlockSpec(memory_space=pltpu.SMEM)
    low = jnp.bfloat16
    return pl.pallas_call(
        grad_kernel,
        grid=(keys // KEY_TILE,),
        out_shape=(
            jax.ShapeDtypeStruct((keys, head_dim), low),
            jax.ShapeDtypeStruct((keys, head_dim), low),
            jax.ShapeDtypeStruct((keys, 2 * head_dim), low),
            jax.ShapeDtypeStruct((rows, 2 * head_dim), low),
        ),
        in_specs=[
            smem,
            smem,
            whole((1, rows)),
            whole(stats.shape),
            whole(every.shape),
            keyed(head_dim),
            keyed(head_dim),
            keyed(2 * head_dim),
        ],
        out_specs=(
            keyed(head_dim),
            keyed(head_dim),
            keyed(2 * head_dim),
            whole((rows, 2 * head_dim)),
        ),
        scratch_shapes=[
            pltpu.VMEM((8, rows), jnp.float32),
            pltpu.VMEM((rows, 2 * head_dim), jnp.float32),
        ],
        compiler_params=VMEM,
        cost_estimate=pl.CostEstimate(
            flops=20 * rows * keys * head_dim,
            bytes_accessed=2 * 4 * head_dim * (rows + 2 * keys),
            transcendentals=2 * rows * keys,
        ),
    )(base, lam, positions, stats, every, k_first, k_second, values)


def spread(value, axes):
    copies = jnp.broadcast_to(value[None], (lax.axis_size(axes),) + value.shape)
    return lax.all_to_all(copies, axes, 0, 0)


def fold_kernel(one_ref, two_ref, out_ref):
    out_ref[...] = jnp.zeros_like(out_ref)
    for row in MAPS:
        one, two = one_ref[row : row + 1, :], two_ref[row : row + 1, :]
        top = jnp.maximum(one, two)
        left, right = jnp.exp(one - top), jnp.exp(two - top)
        out_ref[row : row + 1, :] = top
        for item in (row + 1, row + 2):
            out_ref[item : item + 1, :] = (
                one_ref[item : item + 1, :] * left + two_ref[item : item + 1, :] * right
            )


def fold(one, two):
    return pl.pallas_call(fold_kernel, out_shape=jax.ShapeDtypeStruct(one.shape, one.dtype))(
        one, two
    )


def body(sizes, q_first, q_second, grad_out, k_first, k_second, values, w_query, offsets, lam):
    rows_own, head_dim = q_first.shape
    keys_own = k_first.shape[0]
    y, z, core = (sizes[name] for name in ("y", "z", "core"))
    rows = y * z * core * rows_own
    base = (lax.axis_index(("y", "z", "core")) * keys_own).astype(jnp.int32).reshape(1)
    starts = offsets.reshape(y, z, core).transpose(0, 2, 1).reshape(-1, 1) * rows_own
    positions = (starts + jnp.arange(rows_own, dtype=jnp.int32)[None, :]).reshape(1, rows)

    own = jnp.concatenate([q_first, q_second, grad_out], axis=1)
    every = spread(spread(own, "z"), ("y", "core")).reshape(rows, 4 * head_dim)

    stats = local_stats(base, positions, every, k_first, k_second, values)
    for name in ("core", "y"):
        size = sizes[name]
        reach = 1
        while reach < size:
            pairs = [(i, i ^ reach) for i in range(size)]
            stats = fold(stats, lax.ppermute(stats, name, pairs))
            reach *= 2
    stats = spread(stats, "z")

    dk_first, dk_second, dval, dq = local_grads(
        base, lam, positions, stats, every, k_first, k_second, values
    )

    dq = dq.reshape(y * core, z * rows_own, 2 * head_dim)
    dq = lax.all_to_all(dq, ("y", "core"), 0, 0)
    dq = jnp.sum(dq.astype(jnp.float32), axis=0).astype(jnp.bfloat16)
    dq = lax.all_to_all(dq.reshape(z, rows_own, 2 * head_dim), "z", 0, 0)
    dq = jnp.sum(dq.astype(jnp.float32), axis=0).astype(jnp.bfloat16)

    heads = sizes["head"]
    columns = w_query.reshape(heads, w_query.shape[0] // heads, 2 * head_dim)
    term = jnp.einsum("qe,hde->hqd", dq, columns, preferred_element_type=jnp.float32)
    term = lax.all_to_all(term.astype(jnp.bfloat16), "head", 0, 0)
    slab = jnp.sum(term.astype(jnp.float32), axis=0).astype(jnp.bfloat16)
    return dq[:, :head_dim], dq[:, head_dim:], dk_first, dk_second, dval, slab


def build(mesh, y, z, core):
    names = ("y", "z", "core", "head")
    fine = Mesh(mesh.devices.reshape(y, z, core, mesh.shape["head"]), names)
    sizes = dict(zip(names, fine.devices.shape))
    cut = P(("y", "z", "core"), "head")

    def run(*args):
        return body(sizes, *args)

    return jax.shard_map(
        run,
        mesh=fine,
        in_specs=(cut,) * 6 + (P(None, "head"), P(), P()),
        out_specs=(cut,) * 6,
        check_vma=False,
    )


def solution(mesh):
    return build(mesh, 4, 8, 2)
```

time: 1780 us -> 167 us (0.09)
  the two profiles are of different devices: /device:TPU:24 before, /device:TPU:32 now
where the time goes in v1:
time: 167 us; the launch traced here: 166 us
  waiting for transfers between devices  55.7 us (33%)
  blocking collectives  50.9 us (30%)
  starting transfers between devices  26.5 us (16%)
  Pallas kernels  17.2 us (10%)
  local copies, waits for them, and re-layouts  11.3 us (7%)
  other arithmetic  1.67 us (1%)
    all_to_all x2, waiting for transfers between devices, spread(): return lax.all_to_all(copies, axes, 0, 0)  29.1 us
    all_to_all x1, blocking collectives, spread(): return lax.all_to_all(copies, axes, 0, 0)  23.6 us
    all_to_all x1, waiting for transfers between devices, body(): term = lax.all_to_all(term.astype(jnp.bfloat16), 'head', 0, 0)  16.8 us
    all_to_all x1, blocking collectives, body(): dq = lax.all_to_all(dq.reshape(z, rows_own, 2 * head_dim), 'z', 0, 0)  14.5 us
    all_to_all x1, blocking collectives, body(): dq = lax.all_to_all(dq, ('y', 'core'), 0, 0)  12.8 us
    all_to_all x1, starting transfers between devices, body(): term = lax.all_to_all(term.astype(jnp.bfloat16), 'head', 0, 0)  10 us
    ppermute x3, waiting for transfers between devices, body(): stats = fold(stats, lax.ppermute(stats, name, pairs))  9.69 us
    all_to_all x2, starting transfers between devices, spread(): return lax.all_to_all(copies, axes, 0, 0)  9.55 us
  transfers between devices with their start and end apart: 6, of which 6 were waited for; matrix products, arithmetic and copies ran while one was open for 1% of the time, Pallas kernels for 0%

profile of v1, /device:TPU:32, one launch (start us, length us, event | category | flops | bytes accessed | tf_op | source)
XLA Modules:
  0.0 166.0 jit_solution(11951572344186938240)
XLA Ops:
  1.5 23.6 %all_to_all.30 = bf16[8,16,512]{2,1,0:T(8,128)(2,1)S(1)} all-to-all(bf16[8,16,512]{2,1,0:T(8,128)(2,1)S(1)} %broadcast_in_dim.6), channel_id=1, replica_groups=mesh['y'=4,'z'=8,'core'=2,'head'=8] {'z'}, dimensions={0} | all-to-all | bytes 262144 | tf_op jit(solution)/shard_map/all_to_all | solution.py:218
  25.1 1.1 broadcast_in_dim.7
  26.3 4.5 %all-to-all-start.1 = ((bf16[8,8,16,512]{3,2,1,0:T(8,128)(2,1)}), bf16[8,8,16,512]{3,2,1,0:T(8,128)(2,1)S(1)}, u32[]{:S(2)}, u32[]{:S(2)}) async-start(bf16[8,8,16,512]{3,2,1,0:T(8,128)(2,1)} %broadcast_in_dim.7), calls=%async_computation.1 | async-start | bytes 2097152 | tf_op jit(solution)/shard_map/all_to_all | solution.py:218
  31.2 15.5 %all-to-all-done.1 = bf16[8,8,16,512]{3,2,1,0:T(8,128)(2,1)S(1)} async-done(((bf16[8,8,16,512]{3,2,1,0:T(8,128)(2,1)}), bf16[8,8,16,512]{3,2,1,0:T(8,128)(2,1)S(1)}, u32[]{:S(2)}, u32[]{:S(2)}) %all-to-all-start.1) | async-done | bytes 1048608 | tf_op jit(solution)/shard_map/all_to_all | solution.py:218
  46.7 1.0 copy-done.2
  49.6 4.2 %shard_map.136.one_ref = f32[8,1024]{1,0:T(8,128)S(1)} custom-call(s32[1]{0:T(128)} %bitcast.base_ref, s32[1,1024]{1,0:T(1,128)S(1)} %add.34.pos_ref, bf16[1024,512]{1,0:T(8,128)(2,1)S(1)} %bitcast.13, bf16[1024,128]{1,0:T(8,128)(2,1)S(1)} %copy-done.4, bf16[1024,128]{1,0:T(8,128)(2,1)S(1)} %copy-done.6, bf16[1024,256]{1,0:T(8,128)(2,1)S(1)} %copy-done.2), custom_call_target="tpu_custom_call" | custom-call | flops 1073741824 | bytes 2097152 | tf_op jit(solution)/shard_map/pallas_call | solution.py:152
  53.9 1.9 %collective-permute-start = (f32[8,1024]{1,0:T(8,128)S(1)}, f32[8,1024]{1,0:T(8,128)S(1)}, u32[]{:S(2)}, u32[]{:S(2)}) collective-permute-start(f32[8,1024]{1,0:T(8,128)S(1)} %shard_map.136.one_ref), channel_id=1, source_target_pairs={{0,8},{8,0},{1,9},{9,1},{2,10},{10,2},{3,11},{11,3},{4,12},{12,4},... | collective-permute-start | bytes 98312 | tf_op jit(solution)/shard_map/ppermute | solution.py:258
  55.8 1.2 collective-permute-done.two_ref
  57.6 1.4 shard_map.137.one_ref
  59.0 2.5 %collective-permute-start.1 = (f32[8,1024]{1,0:T(8,128)}, f32[8,1024]{1,0:T(8,128)S(1)}, u32[]{:S(2)}, u32[]{:S(2)}) collective-permute-start(f32[8,1024]{1,0:T(8,128)} %shard_map.137.one_ref), channel_id=1, source_target_pairs={{0,128},{128,0},{256,384},{384,256},{1,129},{129,1},{257,385},{385... | collective-permute-start | bytes 98312 | tf_op jit(solution)/shard_map/ppermute | solution.py:258
  61.5 3.5 %collective-permute-done.1.two_ref = f32[8,1024]{1,0:T(8,128)S(1)} collective-permute-done((f32[8,1024]{1,0:T(8,128)}, f32[8,1024]{1,0:T(8,128)S(1)}, u32[]{:S(2)}, u32[]{:S(2)}) %collective-permute-start.1) | collective-permute-done | bytes 32800 | tf_op jit(solution)/shard_map/ppermute | solution.py:258
  65.7 1.4 shard_map.138.one_ref
  67.1 2.5 %collective-permute-start.2 = (f32[8,1024]{1,0:T(8,128)}, f32[8,1024]{1,0:T(8,128)S(1)}, u32[]{:S(2)}, u32[]{:S(2)}) collective-permute-start(f32[8,1024]{1,0:T(8,128)} %shard_map.138.one_ref), channel_id=1, source_target_pairs={{0,256},{128,384},{256,0},{384,128},{1,257},{129,385},{257,1},{385... | collective-permute-start | bytes 98312 | tf_op jit(solution)/shard_map/ppermute | solution.py:258
  69.6 5.0 %collective-permute-done.2.two_ref = f32[8,1024]{1,0:T(8,128)S(1)} collective-permute-done((f32[8,1024]{1,0:T(8,128)}, f32[8,1024]{1,0:T(8,128)S(1)}, u32[]{:S(2)}, u32[]{:S(2)}) %collective-permute-start.2) | collective-permute-done | bytes 32800 | tf_op jit(solution)/shard_map/ppermute | solution.py:258
  75.2 1.4 shard_map.139
  76.6 1.5 broadcast_in_dim.8
  78.1 5.1 %all-to-all-start.2 = ((f32[8,8,1024]{2,1,0:T(8,128)}), f32[8,8,1024]{2,1,0:T(8,128)S(1)}, u32[]{:S(2)}, u32[]{:S(2)}) async-start(f32[8,8,1024]{2,1,0:T(8,128)} %broadcast_in_dim.8), calls=%async_computation.2 | async-start | bytes 524288 | tf_op jit(solution)/shard_map/all_to_all | solution.py:218
  83.8 13.7 %all-to-all-done.2.stats_ref = f32[8,8,1024]{2,1,0:T(8,128)S(1)} async-done(((f32[8,8,1024]{2,1,0:T(8,128)}), f32[8,8,1024]{2,1,0:T(8,128)S(1)}, u32[]{:S(2)}, u32[]{:S(2)}) %all-to-all-start.2) | async-done | bytes 262176 | tf_op jit(solution)/shard_map/all_to_all | solution.py:218
  100.4 8.8 %shard_map.140 = (bf16[1024,128]{1,0:T(8,128)(2,1)}, bf16[1024,128]{1,0:T(8,128)(2,1)}, bf16[1024,256]{1,0:T(8,128)(2,1)}, bf16[1024,256]{1,0:T(8,128)(2,1)S(1)}) custom-call(s32[1]{0:T(128)} %bitcast.base_ref, f32[1]{0:T(128)S(6)} %copy.18.lam_ref, s32[1,1024]{1,0:T(1,128)S(1)} %add.34.pos_ref, f32[8,8,1024]{2,1,0:T(8,128)S(1)} %all-to-all-done.2.stats_ref, ...), custom_call_target="tpu_custom_call" | custom-call | flops 2684354560 | bytes 3145728 | tf_op jit(solution)/shard_map/pallas_call | solution.py:178
  109.2 12.8 %all_to_all.31 = bf16[8,128,256]{2,1,0:T(8,128)(2,1)S(1)} all-to-all(bf16[8,128,256]{2,1,0:T(8,128)(2,1)S(1)} %bitcast.15), channel_id=1, replica_groups=mesh['y'=4,'z'=8,'core'=2,'head'=8] {'y','core'}, dimensions={0} | all-to-all | bytes 1048576 | tf_op jit(solution)/shard_map/all_to_all | solution.py:267
  122.0 14.5 %all_to_all.32 = bf16[8,16,256]{2,1,0:T(8,128)(2,1)S(1)} all-to-all(bf16[8,16,256]{2,1,0:T(8,128)(2,1)S(1)} %bitcast.16), channel_id=1, replica_groups=mesh['y'=4,'z'=8,'core'=2,'head'=8] {'z'}, dimensions={0} | all-to-all | bytes 131072 | tf_op jit(solution)/shard_map/all_to_all | solution.py:269
  136.6 1.3 fusion
  137.9 10.0 %all-to-all-start.5 = ((bf16[8,16,512]{2,1,0:T(8,128)(2,1)}), bf16[8,16,512]{2,1,0:T(8,128)(2,1)S(1)}, u32[]{:S(2)}, u32[]{:S(2)}) async-start(bf16[8,16,512]{2,1,0:T(8,128)(2,1)} %fusion), calls=%async_computation.5 | async-start | bytes 262144 | tf_op jit(solution)/shard_map/all_to_all | solution.py:275
  148.6 16.8 %all-to-all-done.5 = bf16[8,16,512]{2,1,0:T(8,128)(2,1)S(1)} async-done(((bf16[8,16,512]{2,1,0:T(8,128)(2,1)}), bf16[8,16,512]{2,1,0:T(8,128)(2,1)S(1)}, u32[]{:S(2)}, u32[]{:S(2)}) %all-to-all-start.5) | async-done | bytes 131104 | tf_op jit(solution)/shard_map/all_to_all | solution.py:275
  (35 shorter events, 9.4 us)
Async XLA Ops:
  0.6 136.0 %copy-start = (bf16[4096,256]{1,0:T(8,128)(2,1)S(1)}, bf16[4096,256]{1,0:T(8,128)(2,1)}, u32[]{:S(2)}) copy-start(bf16[4096,256]{1,0:T(8,128)(2,1)} %param.15) | copy-start | bytes 6291460
  0.6 30.1 %copy-start.11 = (s32[64]{0:T(128)S(1)}, s32[64]{0:T(128)}, u32[]{:S(2)}) copy-start(s32[64]{0:T(128)} %param.16) | copy-start | bytes 772
  26.3 20.4 %all-to-all-start.1 = ((bf16[8,8,16,512]{3,2,1,0:T(8,128)(2,1)}), bf16[8,8,16,512]{3,2,1,0:T(8,128)(2,1)S(1)}, u32[]{:S(2)}, u32[]{:S(2)}) async-start(bf16[8,8,16,512]{3,2,1,0:T(8,128)(2,1)} %broadcast_in_dim.7), calls=%async_computation.1 | async-start | bytes 2097152 | tf_op jit(solution)/shard_map/all_to_all | solution.py:218
  46.7 1.0 copy-start.2
  47.7 0.9 copy-start.4
  48.7 0.9 copy-start.6
  53.9 3.1 %copy-start.1 = (f32[8,1024]{1,0:T(8,128)}, f32[8,1024]{1,0:T(8,128)S(1)}, u32[]{:S(2)}) copy-start(f32[8,1024]{1,0:T(8,128)S(1)} %shard_map.136.one_ref) | copy-start | bytes 98308
  53.9 3.1 %collective-permute-start = (f32[8,1024]{1,0:T(8,128)S(1)}, f32[8,1024]{1,0:T(8,128)S(1)}, u32[]{:S(2)}, u32[]{:S(2)}) collective-permute-start(f32[8,1024]{1,0:T(8,128)S(1)} %shard_map.136.one_ref), channel_id=1, source_target_pairs={{0,8},{8,0},{1,9},{9,1},{2,10},{10,2},{3,11},{11,3},{4,12},{12,4},... | collective-permute-start | bytes 98312 | tf_op jit(solution)/shard_map/ppermute | solution.py:258
  57.0 0.6 copy-start.8
  59.0 6.0 %collective-permute-start.1 = (f32[8,1024]{1,0:T(8,128)}, f32[8,1024]{1,0:T(8,128)S(1)}, u32[]{:S(2)}, u32[]{:S(2)}) collective-permute-start(f32[8,1024]{1,0:T(8,128)} %shard_map.137.one_ref), channel_id=1, source_target_pairs={{0,128},{128,0},{256,384},{384,256},{1,129},{129,1},{257,385},{385... | collective-permute-start | bytes 98312 | tf_op jit(solution)/shard_map/ppermute | solution.py:258
  65.0 0.6 copy-start.9
  67.1 7.5 %collective-permute-start.2 = (f32[8,1024]{1,0:T(8,128)}, f32[8,1024]{1,0:T(8,128)S(1)}, u32[]{:S(2)}, u32[]{:S(2)}) collective-permute-start(f32[8,1024]{1,0:T(8,128)} %shard_map.138.one_ref), channel_id=1, source_target_pairs={{0,256},{128,384},{256,0},{384,128},{1,257},{129,385},{257,1},{385... | collective-permute-start | bytes 98312 | tf_op jit(solution)/shard_map/ppermute | solution.py:258
  74.6 0.6 copy-start.10
  78.1 19.4 %all-to-all-start.2 = ((f32[8,8,1024]{2,1,0:T(8,128)}), f32[8,8,1024]{2,1,0:T(8,128)S(1)}, u32[]{:S(2)}, u32[]{:S(2)}) async-start(f32[8,8,1024]{2,1,0:T(8,128)} %broadcast_in_dim.8), calls=%async_computation.2 | async-start | bytes 524288 | tf_op jit(solution)/shard_map/all_to_all | solution.py:218
  97.5 1.0 copy-start.3
  98.5 0.9 copy-start.5
  99.4 0.9 copy-start.7
  137.9 27.5 %all-to-all-start.5 = ((bf16[8,16,512]{2,1,0:T(8,128)(2,1)}), bf16[8,16,512]{2,1,0:T(8,128)(2,1)S(1)}, u32[]{:S(2)}, u32[]{:S(2)}) async-start(bf16[8,16,512]{2,1,0:T(8,128)(2,1)} %fusion), calls=%async_computation.5 | async-start | bytes 262144 | tf_op jit(solution)/shard_map/all_to_all | solution.py:275

commit v2 on v1

v2 whole, which is shorter than its diff:
```python
import jax
import jax.numpy as jnp
from jax import lax
from jax.experimental import pallas as pl
from jax.experimental.pallas import tpu as pltpu
from jax.sharding import Mesh, PartitionSpec as P

NEG = -1e30
KEY_TILE = 256
ROW_TILE = 256
VMEM = pltpu.CompilerParams(vmem_limit_bytes=58 * 1024 * 1024)

STATS = 4


def outer(left, right):
    return lax.dot_general(
        left, right, (((1,), (1,)), ((), ())), preferred_element_type=jnp.float32
    )


def matmul(left, right):
    return jnp.dot(left, right, preferred_element_type=jnp.float32)


def matmul_first(left, right):
    return lax.dot_general(
        left, right, (((0,), (0,)), ((), ())), preferred_element_type=jnp.float32
    )


def tiles(total, size):
    size = min(size, total)
    return [(start, size) for start in range(0, total, size)]


def seen(step, base_ref, pos_ref, span, tile, width):
    key_pos = base_ref[0] + step * tile + lax.broadcasted_iota(jnp.int32, (tile, width), 0)
    return key_pos <= pos_ref[:, span]


def fold(parts_ref, span):
    result = []
    for row in (0, 2):
        logs = [parts_ref[part, row : row + 1, span] for part in range(parts_ref.shape[0])]
        means = [parts_ref[part, row + 1 : row + 2, span] for part in range(parts_ref.shape[0])]
        top = logs[0]
        for item in logs[1:]:
            top = jnp.maximum(top, item)
        total, mix = jnp.zeros_like(top), jnp.zeros_like(top)
        for item, mean in zip(logs, means):
            weight = jnp.exp(item - top)
            total = total + weight
            mix = mix + weight * mean
        result.append((top + jnp.log(total), mix / total))
    return result


def stats_kernel(
    base_ref, pos_ref, every_ref, k_one_ref, k_two_ref, val_ref, stats_ref, run_ref
):
    tile, head_dim = k_one_ref.shape
    scale = head_dim**-0.5
    step = pl.program_id(0)

    @pl.when(step == 0)
    def _():
        row = lax.broadcasted_iota(jnp.int32, run_ref.shape, 0)
        run_ref[...] = jnp.where((row == 0) | (row == 4), NEG, 0.0)

    for start, width in tiles(every_ref.shape[0], ROW_TILE):
        span = slice(start, start + width)
        visible = seen(step, base_ref, pos_ref, span, tile, width)
        product = outer(val_ref[...], every_ref[span, 2 * head_dim :])
        for row, k_ref, offset in ((0, k_one_ref, 0), (4, k_two_ref, head_dim)):
            logits = outer(k_ref[...], every_ref[span, offset : offset + head_dim]) * scale
            logits = jnp.where(visible, logits, NEG)
            before = run_ref[row : row + 1, span]
            top = jnp.maximum(before, jnp.max(logits, axis=0, keepdims=True))
            expo = jnp.exp(logits - top)
            kept = jnp.exp(before - top)
            run_ref[row : row + 1, span] = top
            run_ref[row + 1 : row + 2, span] = run_ref[
                row + 1 : row + 2, span
            ] * kept + jnp.sum(expo, axis=0, keepdims=True)
            run_ref[row + 2 : row + 3, span] = run_ref[
                row + 2 : row + 3, span
            ] * kept + jnp.sum(expo * product, axis=0, keepdims=True)

    @pl.when(step == pl.num_programs(0) - 1)
    def _():
        for row in (0, 4):
            log = run_ref[row : row + 1, :] + jnp.log(run_ref[row + 1 : row + 2, :])
            mean = run_ref[row + 2 : row + 3, :] / run_ref[row + 1 : row + 2, :]
            stats_ref[row // 2 : row // 2 + 1, :] = log
            stats_ref[row // 2 + 1 : row // 2 + 2, :] = mean


def fold_kernel(parts_ref, out_ref):
    (log_one, mean_one), (log_two, mean_two) = fold(parts_ref, slice(None))
    out_ref[0:1, :] = log_one
    out_ref[1:2, :] = mean_one
    out_ref[2:3, :] = log_two
    out_ref[3:4, :] = mean_two


def query_kernel(
    base_ref,
    lam_ref,
    pos_ref,
    far_ref,
    every_ref,
    k_one_ref,
    k_two_ref,
    val_ref,
    out_ref,
    final_ref,
    acc_ref,
):
    tile, head_dim = k_one_ref.shape
    scale = head_dim**-0.5
    step = pl.program_id(0)

    @pl.when(step == 0)
    def _():
        fold_kernel(far_ref, final_ref)
        acc_ref[...] = jnp.zeros_like(acc_ref)

    for start, width in tiles(every_ref.shape[0], ROW_TILE):
        span = slice(start, start + width)
        visible = seen(step, base_ref, pos_ref, span, tile, width)
        product = outer(val_ref[...], every_ref[span, 2 * head_dim :])
        for number, k_ref, factor in ((0, k_one_ref, scale), (1, k_two_ref, -lam_ref[0] * scale)):
            top = number * head_dim
            log = final_ref[2 * number : 2 * number + 1, span]
            mean = final_ref[2 * number + 1 : 2 * number + 2, span]
            logits = outer(k_ref[...], every_ref[span, top : top + head_dim]) * scale
            prob = jnp.exp(jnp.where(visible, logits, NEG) - log)
            slope = (prob * (product - mean) * factor).astype(jnp.bfloat16)
            acc_ref[top : top + head_dim, span] += matmul_first(k_ref[...], slope)

    @pl.when(step == pl.num_programs(0) - 1)
    def _():
        out_ref[...] = acc_ref[...].T.astype(jnp.bfloat16)


def key_kernel(
    base_ref,
    lam_ref,
    pos_ref,
    far_ref,
    every_ref,
    k_one_ref,
    k_two_ref,
    val_ref,
    dk_one_ref,
    dk_two_ref,
    dval_ref,
    final_ref,
):
    tile, head_dim = k_one_ref.shape
    scale = head_dim**-0.5
    step = pl.program_id(0)
    lam = lam_ref[0]

    @pl.when(step == 0)
    def _():
        fold_kernel(far_ref, final_ref)

    grad_one = jnp.zeros((tile, head_dim), jnp.float32)
    grad_two = jnp.zeros((tile, head_dim), jnp.float32)
    grad_val = jnp.zeros((tile, 2 * head_dim), jnp.float32)
    for start, width in tiles(every_ref.shape[0], ROW_TILE):
        span = slice(start, start + width)
        visible = seen(step, base_ref, pos_ref, span, tile, width)
        q_one = every_ref[span, :head_dim]
        q_two = every_ref[span, head_dim : 2 * head_dim]
        cotangent = every_ref[span, 2 * head_dim :]
        product = outer(val_ref[...], cotangent)
        logits_one = jnp.where(visible, outer(k_one_ref[...], q_one) * scale, NEG)
        logits_two = jnp.where(visible, outer(k_two_ref[...], q_two) * scale, NEG)
        prob_one = jnp.exp(logits_one - final_ref[0:1, span])
        prob_two = jnp.exp(logits_two - final_ref[2:3, span]) * lam
        mixed = (prob_one - prob_two).astype(jnp.bfloat16)
        slope_one = (prob_one * (product - final_ref[1:2, span]) * scale).astype(jnp.bfloat16)
        slope_two = (prob_two * (final_ref[3:4, span] - product) * scale).astype(jnp.bfloat16)
        grad_val = grad_val + matmul(mixed, cotangent)
        grad_one = grad_one + matmul(slope_one, q_one)
        grad_two = grad_two + matmul(slope_two, q_two)
    dk_one_ref[...] = grad_one.astype(jnp.bfloat16)
    dk_two_ref[...] = grad_two.astype(jnp.bfloat16)
    dval_ref[...] = grad_val.astype(jnp.bfloat16)


def whole(shape):
    return pl.BlockSpec(shape, lambda step: (0,) * len(shape))


def keyed(width):
    return pl.BlockSpec((KEY_TILE, width), lambda step: (step, 0))


SMEM = pl.BlockSpec(memory_space=pltpu.SMEM)


def over_keys(kernel, scalars, fixed, keyed_in, fixed_out, keyed_out, scratch, flops):
    keys = keyed_in[0].shape[0]
    outs = fixed_out + tuple(jax.ShapeDtypeStruct((keys, w), jnp.bfloat16) for w in keyed_out)
    return pl.pallas_call(
        kernel,
        grid=(keys // KEY_TILE,),
        out_shape=outs,
        in_specs=[SMEM] * len(scalars)
        + [whole(item.shape) for item in fixed]
        + [keyed(item.shape[1]) for item in keyed_in],
        out_specs=tuple(whole(item.shape) for item in fixed_out)
        + tuple(keyed(w) for w in keyed_out),
        scratch_shapes=[pltpu.VMEM(shape, jnp.float32) for shape in scratch],
        compiler_params=VMEM,
        cost_estimate=pl.CostEstimate(
            flops=flops, bytes_accessed=4 * 1024 * 1024, transcendentals=flops // 512
        ),
    )(*scalars, *fixed, *keyed_in)


def spread(value, axes):
    copies = jnp.broadcast_to(value[None], (lax.axis_size(axes),) + value.shape)
    return lax.all_to_all(copies, axes, 0, 0)


def body(sizes, q_first, q_second, grad_out, k_first, k_second, values, w_query, offsets, lam):
    rows_own, head_dim = q_first.shape
    keys_own = k_first.shape[0]
    y, z, core = (sizes[name] for name in ("y", "z", "core"))
    rows = y * z * core * rows_own
    base = (lax.axis_index(("y", "z", "core")) * keys_own).astype(jnp.int32).reshape(1)
    starts = offsets.reshape(y, z, core).transpose(0, 2, 1).reshape(-1, 1) * rows_own
    positions = (starts + jnp.arange(rows_own, dtype=jnp.int32)[None, :]).reshape(1, rows)

    own = jnp.concatenate([q_first, q_second, grad_out], axis=1)
    every = spread(lax.all_gather(own, "z"), ("y", "core")).reshape(rows, 4 * head_dim)

    held = (k_first, k_second, values)
    pairs = rows * keys_own * head_dim
    stats_of = jax.ShapeDtypeStruct((STATS, rows), jnp.float32)
    (stats,) = over_keys(
        stats_kernel, (base,), (positions, every), held, (stats_of,), (), [(8, rows)], 8 * pairs
    )
    stats = lax.all_gather(stats, ("y", "core"))
    stats = pl.pallas_call(fold_kernel, out_shape=stats_of, compiler_params=VMEM)(stats)
    stats = lax.all_gather(stats, "z")
    (dq,) = over_keys(
        query_kernel,
        (base, lam),
        (positions, stats, every),
        held,
        (jax.ShapeDtypeStruct((rows, 2 * head_dim), jnp.bfloat16),),
        (),
        [(STATS, rows), (2 * head_dim, rows)],
        12 * pairs,
    )
    dq = dq.reshape(y * core, z * rows_own, 2 * head_dim)
    dq = lax.all_to_all(dq, ("y", "core"), 0, 0)
    dk_first, dk_second, dval = over_keys(
        key_kernel,
        (base, lam),
        (positions, stats, every),
        held,
        (),
        (head_dim, head_dim, 2 * head_dim),
        [(STATS, rows)],
        16 * pairs,
    )
    dq = jnp.sum(dq.astype(jnp.float32), axis=0).astype(jnp.bfloat16)
    dq = lax.all_to_all(dq.reshape(z, rows_own, 2 * head_dim), "z", 0, 0)
    dq = jnp.sum(dq.astype(jnp.float32), axis=0).astype(jnp.bfloat16)

    heads = sizes["head"]
    columns = w_query.reshape(heads, w_query.shape[0] // heads, 2 * head_dim)
    term = jnp.einsum("qe,hde->hqd", dq, columns, preferred_element_type=jnp.float32)
    term = lax.all_to_all(term.astype(jnp.bfloat16), "head", 0, 0)
    slab = jnp.sum(term.astype(jnp.float32), axis=0).astype(jnp.bfloat16)
    return dq[:, :head_dim], dq[:, head_dim:], dk_first, dk_second, dval, slab


def build(mesh, y, z, core):
    names = ("y", "z", "core", "head")
    fine = Mesh(mesh.devices.reshape(y, z, core, mesh.shape["head"]), names)
    sizes = dict(zip(names, fine.devices.shape))
    cut = P(("y", "z", "core"), "head")

    def run(*args):
        return body(sizes, *args)

    return jax.shard_map(
        run,
        mesh=fine,
        in_specs=(cut,) * 6 + (P(None, "head"), P(), P()),
        out_specs=(cut,) * 6,
        check_vma=False,
    )


def solution(mesh):
    return build(mesh, 4, 8, 2)
```

time: 167 us -> 215 us (1.29)
  blocking collectives: 50.9 us -> 144 us
  waiting for transfers between devices: 55.7 us -> 22.9 us
  starting transfers between devices: 26.5 us -> 14.5 us
  local copies, waits for them, and re-layouts: 11.3 us -> 3.69 us
  Pallas kernels: 17.2 us -> 24.2 us
    all_gather x0 -> x3, blocking collectives: none -> 112 us  [the longest x1 49.1 us: body(): lax.all_gather(own, 'z')]
    all_to_all x1 -> x0, blocking collectives: 23.6 us -> none  [spread(): return lax.all_to_all(copies, axes, 0, 0)]
    all_to_all x2 -> x1, waiting for transfers between devices: 29.1 us -> 14.2 us  [spread(): return lax.all_to_all(copies, axes, 0, 0)]
    ppermute x3 -> x0, waiting for transfers between devices: 9.69 us -> none  [body(): stats = fold(stats, lax.ppermute(stats, name, pairs))]
    all_to_all x1, waiting for transfers between devices: 16.8 us -> 8.68 us  [body(): term = lax.all_to_all(term.astype(jnp.bfloat16), 'head', 0, 0)]
    pallas_call x5 -> x4, Pallas kernels: 17.2 us -> 24.2 us  [the longest x3 22.6 us: over_keys(): pl.pallas_call(kernel, grid=(keys // KEY_TILE,), out_shape=outs, in_specs...]
    ppermute x3 -> x0, starting transfers between devices: 6.9 us -> none  [body(): stats = fold(stats, lax.ppermute(stats, name, pairs))]
    unnamed x24 -> x6, local copies, waits for them, and re-layouts: 7.74 us -> 1 us
  transfers between devices with their start and end apart: 6 -> 2, of which waited for: 6 -> 2; matrix products, arithmetic and copies ran while one was open for 1% -> 1% of each run, Pallas kernels for 0% -> 4%
where the time goes in v2:
time: 215 us; the launch traced here: 214 us
  blocking collectives  144 us (67%)
  Pallas kernels  24.2 us (11%)
  waiting for transfers between devices  22.9 us (11%)
  starting transfers between devices  14.5 us (7%)
  local copies, waits for them, and re-layouts  3.69 us (2%)
    all_gather x1, blocking collectives, body(): lax.all_gather(own, 'z')  49.1 us
    all_gather x1, blocking collectives, body(): stats = lax.all_gather(stats, 'z')  48.5 us
    pallas_call x3, Pallas kernels, over_keys(): pl.pallas_call(kernel, grid=(keys // KEY_TILE,), out_shape=outs, in_specs...  22.6 us
    all_to_all x1, blocking collectives, body(): dq = lax.all_to_all(dq.reshape(z, rows_own, 2 * head_dim), 'z', 0, 0)  19 us
    all_to_all x1, waiting for transfers between devices, spread(): return lax.all_to_all(copies, axes, 0, 0)  14.2 us
    all_gather x1, blocking collectives, body(): stats = lax.all_gather(stats, ('y', 'core'))  14 us
    all_to_all x1, blocking collectives, body(): dq = lax.all_to_all(dq, ('y', 'core'), 0, 0)  13.8 us
    all_to_all x1, starting transfers between devices, body(): term = lax.all_to_all(term.astype(jnp.bfloat16), 'head', 0, 0)  10.1 us
  transfers between devices with their start and end apart: 2, of which 2 were waited for; matrix products, arithmetic and copies ran while one was open for 1% of the time, Pallas kernels for 4%

profile of v2, /device:TPU:32, one launch (start us, length us, event | category | flops | bytes accessed | tf_op | source)
XLA Modules:
  0.0 214.1 jit_solution(9356584348573578420)
XLA Ops:
  0.7 0.9 pad_maximum_fusion
  1.5 49.1 %all-gather = bf16[128,512]{1,0:T(8,128)(2,1)S(1)} all-gather(bf16[16,512]{1,0:T(8,128)(2,1)S(1)} %pad_maximum_fusion), channel_id=2, replica_groups=mesh['y'=4,'z'=8,'core'=2,'head'=8] {'z'}, dimensions={0}, use_global_device_ids=true | all-gather | bytes 147456 | tf_op jit(solution)/shard_map/all_gather | solution.py:241
  50.6 1.1 broadcast_in_dim.2
  51.7 4.5 %all-to-all-start = ((bf16[8,8,16,512]{3,2,1,0:T(8,128)(2,1)}), bf16[8,8,16,512]{3,2,1,0:T(8,128)(2,1)S(1)}, u32[]{:S(2)}, u32[]{:S(2)}) async-start(bf16[8,8,16,512]{3,2,1,0:T(8,128)(2,1)} %broadcast_in_dim.2), calls=%async_computation | async-start | bytes 2097152 | tf_op jit(solution)/shard_map/all_to_all | solution.py:228
  56.9 0.1 mul.34
  57.0 0.1 copy.18
  57.1 0.1 mul.36
  57.2 0.1 iota_add_fusion
  57.3 0.7 add.34.pos_ref
  58.0 14.2 %all-to-all-done = bf16[8,8,16,512]{3,2,1,0:T(8,128)(2,1)S(1)} async-done(((bf16[8,8,16,512]{3,2,1,0:T(8,128)(2,1)}), bf16[8,8,16,512]{3,2,1,0:T(8,128)(2,1)S(1)}, u32[]{:S(2)}, u32[]{:S(2)}) %all-to-all-start) | async-done | bytes 1048608 | tf_op jit(solution)/shard_map/all_to_all | solution.py:228
  72.2 1.0 copy-done.1
  73.2 6.4 %shard_map.136 = f32[4,1024]{1,0:T(4,128)} custom-call(s32[1]{0:T(128)} %bitcast.base_ref, s32[1,1024]{1,0:T(1,128)} %add.34.pos_ref, bf16[1024,512]{1,0:T(8,128)(2,1)} %bitcast.16, bf16[1024,128]{1,0:T(8,128)(2,1)} %k_one_ref.5, bf16[1024,128]{1,0:T(8,128)(2,1)} %k_two_ref.5, bf16[1024,256]{1,0:T(8,128)(2,1)} %val_ref.5), custom_call_target="tpu_custom_call" | custom-call | flops 1073741824 | bytes 4194304 | tf_op jit(solution)/shard_map/pallas_call | solution.py:209
  79.6 14.0 %all-gather.3.parts_ref = f32[8,4,1024]{2,1,0:T(4,128)} all-gather(f32[1,4,1024]{2,1,0:T(4,128)} %bitcast.24), channel_id=3, replica_groups=mesh['y'=4,'z'=8,'core'=2,'head'=8] {'y','core'}, dimensions={0}, use_global_device_ids=true | all-gather | bytes 147456 | tf_op jit(solution)/shard_map/all_gather | solution.py:249
  93.6 1.5 shard_map.137
  95.1 48.5 %all-gather.4.far_ref = f32[8,4,1024]{2,1,0:T(4,128)} all-gather(f32[1,4,1024]{2,1,0:T(4,128)} %bitcast.22), channel_id=4, replica_groups=mesh['y'=4,'z'=8,'core'=2,'head'=8] {'z'}, dimensions={0}, use_global_device_ids=true | all-gather | bytes 147456 | tf_op jit(solution)/shard_map/all_gather | solution.py:251
  143.7 8.1 %shard_map.138 = bf16[1024,256]{1,0:T(8,128)(2,1)} custom-call(s32[1]{0:T(128)} %bitcast.base_ref, f32[1]{0:T(128)S(6)} %copy.19.lam_ref, s32[1,1024]{1,0:T(1,128)} %add.34.pos_ref, f32[8,4,1024]{2,1,0:T(4,128)} %all-gather.4.far_ref, bf16[1024,512]{1,0:T(8,128)(2,1)} %bitcast.17, bf16[1024,128]{1,0:T(8,128)(2,1)} %k_one_ref.5, bf16[1024,128]{1,0:T(8,128)(2,1)} %k_two_ref.5, ...), custom_call_target="tpu_custom_call" | custom-call | flops 1610612736 | bytes 4194304 | tf_op jit(solution)/shard_map/pallas_call | solution.py:209
  151.7 13.8 %all_to_all.20 = bf16[8,128,256]{2,1,0:T(8,128)(2,1)S(1)} all-to-all(bf16[8,128,256]{2,1,0:T(8,128)(2,1)} %bitcast.20), channel_id=1, replica_groups=mesh['y'=4,'z'=8,'core'=2,'head'=8] {'y','core'}, dimensions={0} | all-to-all | bytes 1048576 | tf_op jit(solution)/shard_map/all_to_all | solution.py:263
  165.6 19.0 %all_to_all.21 = bf16[8,16,256]{2,1,0:T(8,128)(2,1)S(1)} all-to-all(bf16[8,16,256]{2,1,0:T(8,128)(2,1)S(1)} %bitcast.21), channel_id=1, replica_groups=mesh['y'=4,'z'=8,'core'=2,'head'=8] {'z'}, dimensions={0} | all-to-all | bytes 131072 | tf_op jit(solution)/shard_map/all_to_all | solution.py:275
  184.6 1.3 fusion
  185.9 10.1 %all-to-all-start.3 = ((bf16[8,16,512]{2,1,0:T(8,128)(2,1)}), bf16[8,16,512]{2,1,0:T(8,128)(2,1)S(1)}, u32[]{:S(2)}, u32[]{:S(2)}) async-start(bf16[8,16,512]{2,1,0:T(8,128)(2,1)} %fusion), calls=%async_computation.3 | async-start | bytes 262144 | tf_op jit(solution)/shard_map/all_to_all | solution.py:281
  196.0 8.2 %shard_map.139 = (bf16[1024,128]{1,0:T(8,128)(2,1)}, bf16[1024,128]{1,0:T(8,128)(2,1)}, bf16[1024,256]{1,0:T(8,128)(2,1)}) custom-call(s32[1]{0:T(128)} %bitcast.base_ref, f32[1]{0:T(128)S(6)} %copy.19.lam_ref, s32[1,1024]{1,0:T(1,128)} %add.34.pos_ref, f32[8,4,1024]{2,1,0:T(4,128)} %all-gather.4.far_ref, bf16[1024,512]{1,0:T(8,128)(2,1)} %bitcast.18, ...), custom_call_target="tpu_custom_call" | custom-call | flops 2147483648 | bytes 4194304 | tf_op jit(solution)/shard_map/pallas_call | solution.py:209
  204.2 0.6 fusion.2
  204.8 8.7 %all-to-all-done.3 = bf16[8,16,512]{2,1,0:T(8,128)(2,1)S(1)} async-done(((bf16[8,16,512]{2,1,0:T(8,128)(2,1)}), bf16[8,16,512]{2,1,0:T(8,128)(2,1)S(1)}, u32[]{:S(2)}, u32[]{:S(2)}) %all-to-all-start.3) | async-done | bytes 131104 | tf_op jit(solution)/shard_map/all_to_all | solution.py:281
  213.4 0.6 reduce_sum.38
  (8 shorter events, 0.1 us)
Async XLA Ops:
  0.6 184.0 %copy-start = (bf16[4096,256]{1,0:T(8,128)(2,1)S(1)}, bf16[4096,256]{1,0:T(8,128)(2,1)}, u32[]{:S(2)}) copy-start(bf16[4096,256]{1,0:T(8,128)(2,1)} %param.15) | copy-start | bytes 6291460
  0.6 56.2 %copy-start.2 = (s32[64]{0:T(128)S(1)}, s32[64]{0:T(128)}, u32[]{:S(2)}) copy-start(s32[64]{0:T(128)} %param.16) | copy-start | bytes 772
  51.7 20.5 %all-to-all-start = ((bf16[8,8,16,512]{3,2,1,0:T(8,128)(2,1)}), bf16[8,8,16,512]{3,2,1,0:T(8,128)(2,1)S(1)}, u32[]{:S(2)}, u32[]{:S(2)}) async-start(bf16[8,8,16,512]{3,2,1,0:T(8,128)(2,1)} %broadcast_in_dim.2), calls=%async_computation | async-start | bytes 2097152 | tf_op jit(solution)/shard_map/all_to_all | solution.py:228
  72.2 1.0 copy-start.1
  185.9 27.5 %all-to-all-start.3 = ((bf16[8,16,512]{2,1,0:T(8,128)(2,1)}), bf16[8,16,512]{2,1,0:T(8,128)(2,1)S(1)}, u32[]{:S(2)}, u32[]{:S(2)}) async-start(bf16[8,16,512]{2,1,0:T(8,128)(2,1)} %fusion), calls=%async_computation.3 | async-start | bytes 262144 | tf_op jit(solution)/shard_map/all_to_all | solution.py:281
